TPU v7x, 512 devices: a whole 4x8x8 slice. The times are simulated.
512 devices in a mesh: row: 64 (over y, z), col: 8 (over x, core).
Axes of the slice: x: 4, y: 8, z: 8, core: 2. Of those that a mesh axis runs over, the one named last changes fastest.
Arguments:
- features: bfloat16 [65536, 512], P(('row', 'col')), may hold values from -6 to 6
- weight: bfloat16 [512, 512], replicated, may hold values from -0.25 to 0.25
- bias_vec: float32 [512], replicated, may hold values from -3 to 3
- tile_vals: bfloat16 [64, 8, 16, 128, 128], P('row', 'col'), may hold values from -0.1875 to 0.1875
- tile_coords: int32 [64, 8, 16, 2], P('row', 'col'), may hold values from 0 to 63, as said below
- tile_count: int32 [64, 8], P('row', 'col'), may hold values from 2 to 16, as said below
- cotangent: bfloat16 [65536, 512], P(('row', 'col')), may hold values from -6 to 6
Outputs:
- layer_out: bfloat16 [65536, 512], P(('row', 'col'))
- grad_weight: float32 [512, 512], replicated
- grad_bias: float32 [512], replicated
- grad_features: bfloat16 [65536, 512], P(('row', 'col'))
Inputs may be any that keep to these rules, and one draw needn't show every extreme that they name: tile_coords[r, c, s, 0] is below 8; tile_coords[r, c, s, 1] lies in the row bands r - 3 to r + 3 that exist. `tile_count`: some device has all 16 slots live.
All inputs are finite; a program needn't handle non-finite values.
Results may differ from a plain program's by a relative error of at most 0.019.
Values may be sent and summed in bfloat16 or wider, within the bound.
No kernel may reach another device: no remote copies, remote signals or barrier semaphores. Data moves between devices by JAX's collectives and lax.ppermute only.
A program may use at most 64 MiB of HBM per device.

v0:
```python
import jax
import jax.numpy as jnp
from jax import lax
from jax.sharding import PartitionSpec as P

REACH = 3


def passed_along(block, axis, distance):
    devices = range(lax.axis_size(axis))
    route = [(i - distance, i) for i in devices if i - distance in devices]
    return lax.ppermute(block, axis, route)


def gelu_tanh(values):
    return jax.nn.gelu(values, approximate=True)


def body(features, weight, bias_vec, tile_vals, tile_coords, tile_count, cotangent):
    col_count = lax.axis_size("col")
    own_row = lax.axis_index("row")
    tiles_here = tile_vals[0, 0]
    coords_here = tile_coords[0, 0]
    live_count = tile_count[0, 0]
    slot_count = tiles_here.shape[0]
    tile_size = features.shape[0]
    feat_width = features.shape[1]
    window = 2 * REACH + 1
    per_step = 8
    row_local = coords_here[:, 0]
    col_local = coords_here[:, 1]
    alive_mask = (jnp.arange(slot_count, dtype=jnp.int32) < live_count).astype(jnp.float32)
    window_index = col_local - own_row + REACH
    nearby = []
    for shift_by in range(-REACH, REACH + 1):
        if shift_by == 0:
            nearby.append(features)
        else:
            nearby.append(passed_along(features, "row", -shift_by))
    panels = jnp.stack(nearby)
    step_total = slot_count // per_step

    def slot_slices(group_idx):
        first_slot = group_idx * per_step
        tiles_now = lax.dynamic_slice_in_dim(tiles_here, first_slot, per_step, 0)
        alive_now = lax.dynamic_slice_in_dim(alive_mask, first_slot, per_step, 0)
        return (first_slot, tiles_now, alive_now)

    def forward_group(group_idx, totals):
        first_slot, tiles_now, alive_now = slot_slices(group_idx)
        col_pick = lax.dynamic_slice_in_dim(window_index, first_slot, per_step, 0)
        row_pick = lax.dynamic_slice_in_dim(row_local, first_slot, per_step, 0)
        picked = panels[col_pick]
        product = jnp.einsum("gij,gjf->gif", tiles_now, picked, preferred_element_type=jnp.float32)
        onehot = (row_pick[:, None] == jnp.arange(col_count, dtype=jnp.int32)[None, :]).astype(
            jnp.float32
        )
        onehot = onehot * alive_now[:, None]
        return totals + jnp.einsum("gb,gif->bif", onehot, product)

    partial_value = lax.fori_loop(
        0, step_total, forward_group, jnp.zeros((col_count, tile_size, feat_width), jnp.float32)
    )
    aggregate = lax.psum_scatter(
        partial_value.reshape(col_count * tile_size, feat_width),
        "col",
        scatter_dimension=0,
        tiled=True,
    )
    aggregate_b = aggregate.astype(jnp.bfloat16)
    pre_act = jnp.dot(aggregate_b, weight, preferred_element_type=jnp.float32) + bias_vec
    layer_out = gelu_tanh(pre_act).astype(jnp.bfloat16)
    unused_out, pullback = jax.vjp(gelu_tanh, pre_act)
    grad_pre = pullback(cotangent.astype(jnp.float32))[0].astype(jnp.bfloat16)
    weight_term = jnp.einsum("nf,ng->fg", aggregate_b, grad_pre, preferred_element_type=jnp.float32)
    bias_term = jnp.sum(grad_pre.astype(jnp.float32), axis=0)
    grad_weight, grad_bias = lax.psum((weight_term, bias_term), ("row", "col"))
    grad_mid = jnp.einsum("ng,fg->nf", grad_pre, weight, preferred_element_type=jnp.float32).astype(
        jnp.bfloat16
    )
    band_panels = lax.all_gather(grad_mid, "col", axis=0, tiled=True).reshape(
        col_count, tile_size, feat_width
    )

    def backward_group(group_idx, totals):
        first_slot, tiles_now, alive_now = slot_slices(group_idx)
        row_pick = lax.dynamic_slice_in_dim(row_local, first_slot, per_step, 0)
        win_pick = lax.dynamic_slice_in_dim(window_index, first_slot, per_step, 0)
        picked = band_panels[row_pick]
        product = jnp.einsum("gji,gjf->gif", tiles_now, picked, preferred_element_type=jnp.float32)
        onehot = (win_pick[:, None] == jnp.arange(window, dtype=jnp.int32)[None, :]).astype(
            jnp.float32
        )
        onehot = onehot * alive_now[:, None]
        return totals + jnp.einsum("gb,gif->bif", onehot, product)

    grad_acc = lax.fori_loop(
        0, step_total, backward_group, jnp.zeros((window, tile_size, feat_width), jnp.float32)
    )
    result_sum = grad_acc[REACH]
    for shift_by in range(-REACH, REACH + 1):
        if shift_by != 0:
            result_sum = result_sum + passed_along(grad_acc[shift_by + REACH], "row", shift_by)
    grad_features = result_sum.astype(jnp.bfloat16)
    return (layer_out, grad_weight, grad_bias, grad_features)


def solution(mesh):
    return jax.shard_map(
        body,
        mesh=mesh,
        in_specs=(
            P(("row", "col"), None),
            P(),
            P(),
            P("row", "col", None, None, None),
            P("row", "col", None, None),
            P("row", "col"),
            P(("row", "col"), None),
        ),
        out_specs=(P(("row", "col"), None), P(), P(), P(("row", "col"), None)),
        check_vma=False,
    )
```

profile of v0, /device:TPU:24, one launch (start us, length us, event | category | flops | bytes accessed | tf_op | source)
XLA Modules:
  0.0 473.3 jit_solution(12974934062237815644)
XLA Ops:
  7.2 8.0 %collective-permute-start = (bf16[128,512]{1,0:T(8,128)(2,1)}, bf16[128,512]{1,0:T(8,128)(2,1)S(1)}, u32[]{:S(2)}, u32[]{:S(2)}) collective-permute-start(bf16[128,512]{1,0:T(8,128)(2,1)} %param.11), channel_id=1, source_target_pairs={{0,24},{8,32},{16,40},{24,48},{32,56},{40,64},{48,72},{56,80},{64,... | collective-permute-start | bytes 393224 | tf_op jit(solution)/shard_map/ppermute | solution.py:12
  15.3 6.4 %collective-permute-start.1 = (bf16[128,512]{1,0:T(8,128)(2,1)}, bf16[128,512]{1,0:T(8,128)(2,1)S(1)}, u32[]{:S(2)}, u32[]{:S(2)}) collective-permute-start(bf16[128,512]{1,0:T(8,128)(2,1)} %param.11), channel_id=1, source_target_pairs={{0,16},{8,24},{16,32},{24,40},{32,48},{40,56},{48,64},{56,72},{64,... | collective-permute-start | bytes 393224 | tf_op jit(solution)/shard_map/ppermute | solution.py:12
  21.7 3.4 collective-permute-start.2
  25.1 4.6 collective-permute-start.3
  29.6 1.9 collective-permute-start.4
  31.6 0.8 add_bitcast_fusion
  33.0 4.2 collective-permute-start.5
  37.3 0.9 bitcast_dynamic-update-slice_fusion.3
  38.2 2.6 collective-permute-done.4
  40.9 11.6 %collective-permute-done.5 = bf16[128,512]{1,0:T(8,128)(2,1)S(1)} collective-permute-done((bf16[128,512]{1,0:T(8,128)(2,1)}, bf16[128,512]{1,0:T(8,128)(2,1)S(1)}, u32[]{:S(2)}, u32[]{:S(2)}) %collective-permute-start.5) | collective-permute-done | bytes 131104 | tf_op jit(solution)/shard_map/ppermute | solution.py:12
  52.5 10.2 %while.28 = (s32[]{:T(128)}, f32[8,128,512]{2,0,1:T(8,128)}, s32[16]{0:T(128)S(1)}, bf16[16]{0:T(256)(128)(2,1)S(1)}, bf16[16,128,128]{2,1,0:T(8,128)(2,1)}, /*i...) while((s32[]{:T(128)}, f32[8,128,512]{2,0,1:T(8,128)}, ...), condition=%wide.region_1.0_spmd.clone, body=%wide.region_0.0_spmd.clone.sunk | while | flops 143656096 | bytes 9703877 | solution.py:61
  52.5 0.1 compare_select_fusion.4
  52.6 0.6 gather_fusion
  53.2 1.4 fusion.67
  54.6 0.1 dynamic_slice.80
  54.7 2.1 select_add_fusion.4
  56.9 0.6 gather_fusion
  57.5 1.4 fusion.67
  58.9 0.1 dynamic_slice.80
  59.1 3.7 select_add_fusion.4
  62.7 4.1 copy.18
  67.0 33.2 %reduce-scatter.2.cloned.1.call-done = f32[128,512]{1,0:T(8,128)} async-done(((f32[1024,512]{1,0:T(8,128)}), f32[128,512]{1,0:T(8,128)}) %reduce-scatter.2.cloned.1.call-update) | async-done | bytes 262160 | tf_op jit(solution)/shard_map/reduce_scatter | solution.py:64
  100.2 2.0 convert_reduce_fusion
  102.2 1.0 convolution_convert_fusion
  103.2 27.5 %all-gather.2.cloned.1.call-done = bf16[1024,512]{1,0:T(8,128)(2,1)} async-done(((bf16[128,512]{1,0:T(8,128)(2,1)}), bf16[1024,512]{1,0:T(8,128)(2,1)}) %all-gather.2.cloned.1.call-update) | async-done | bytes 1048592 | tf_op jit(solution)/shard_map/all_gather | solution.py:81
  130.8 11.0 %while.29 = (s32[]{:T(128)}, f32[7,128,512]{2,0,1:T(8,128)}, s32[16]{0:T(128)S(1)}, bf16[16]{0:T(256)(128)(2,1)S(1)}, bf16[16,128,128]{2,1,0:T(8,128)(2,1)S(1)},...) while((s32[]{:T(128)}, f32[7,128,512]{2,0,1:T(8,128)}, ...), condition=%wide.region_7.0_spmd.clone, body=%wide.region_6.0_spmd.clone.sunk | while | flops 142476432 | bytes 9179589 | solution.py:97
  130.9 1.8 gather_fusion.1
  132.7 0.5 fusion.72
  133.2 0.1 dynamic_slice.84
  133.4 2.1 select_add_fusion.5
  135.6 1.8 gather_fusion.1
  137.4 0.5 fusion.72
  137.9 0.1 dynamic_slice.84
  138.1 3.7 select_add_fusion.5
  141.8 2.7 copy.19
  144.5 1.0 slice_bitcast_fusion.5
  145.4 4.6 collective-permute-start.10
  150.1 6.0 %collective-permute-start.11 = (f32[128,512]{1,0:T(8,128)}, f32[128,512]{1,0:T(8,128)S(1)}, u32[]{:S(2)}, u32[]{:S(2)}) collective-permute-start(f32[128,512]{1,0:T(8,128)} %get-tuple-element.333), channel_id=1, source_target_pairs={{0,24},{8,32},{16,40},{24,48},{32,56},{40,64},{48,72},{56,80},{64,... | collective-permute-start | bytes 786440 | tf_op jit(solution)/shard_map/ppermute | solution.py:12
  156.1 3.7 collective-permute-start.6
  159.8 3.3 collective-permute-start.7
  163.2 3.7 collective-permute-start.8
  166.9 1.6 collective-permute-done.10
  168.5 3.8 collective-permute-start.9
  172.4 1.3 fusion.43
  173.7 123.1 %psum.15 = f32[512]{0:T(512)} all-reduce(f32[512]{0:T(512)S(1)} %get-tuple-element.330), channel_id=1, replica_groups=mesh['row'=64,'col'=8] {'row','col'}, use_global_device_ids=true, to_apply=%region_5.0 | all-reduce | flops 512 | bytes 4096 | tf_op jit(solution)/shard_map/psum | solution.py:77
  296.9 2.0 fusion.42
  298.9 165.6 %all-reduce.2.cloned.1.call-done = f32[512,512]{1,0:T(8,128)} async-done(((f32[512,512]{1,0:T(8,128)}), f32[512,512]{1,0:T(8,128)}) %all-reduce.2.cloned.1.call-update) | async-done | bytes 1048592 | tf_op jit(solution)/shard_map/psum | solution.py:77
  464.5 2.3 copy.60
  (45 shorter events, 0.8 us)
Async XLA Ops:
  7.2 93.0 %copy-start = (bf16[512,512]{1,0:T(8,128)(2,1)S(1)}, bf16[512,512]{1,0:T(8,128)(2,1)}, u32[]{:S(2)}) copy-start(bf16[512,512]{1,0:T(8,128)(2,1)} %param.12) | copy-start | bytes 1572868
  7.2 93.0 %reduce-scatter.2.cloned.1.call-start = ((), (), s32[]{:S(2)}) async-start(), calls=%async_computation.1 | async-start | bytes 2359296 | tf_op jit(solution)/shard_map/reduce_scatter | solution.py:64
  7.2 25.8 %collective-permute-start = (bf16[128,512]{1,0:T(8,128)(2,1)}, bf16[128,512]{1,0:T(8,128)(2,1)S(1)}, u32[]{:S(2)}, u32[]{:S(2)}) collective-permute-start(bf16[128,512]{1,0:T(8,128)(2,1)} %param.11), channel_id=1, source_target_pairs={{0,24},{8,32},{16,40},{24,48},{32,56},{40,64},{48,72},{56,80},{64,... | collective-permute-start | bytes 393224 | tf_op jit(solution)/shard_map/ppermute | solution.py:12
  15.3 22.0 %collective-permute-start.1 = (bf16[128,512]{1,0:T(8,128)(2,1)}, bf16[128,512]{1,0:T(8,128)(2,1)S(1)}, u32[]{:S(2)}, u32[]{:S(2)}) collective-permute-start(bf16[128,512]{1,0:T(8,128)(2,1)} %param.11), channel_id=1, source_target_pairs={{0,16},{8,24},{16,32},{24,40},{32,48},{40,56},{48,64},{56,72},{64,... | collective-permute-start | bytes 393224 | tf_op jit(solution)/shard_map/ppermute | solution.py:12
  21.7 15.6 %collective-permute-start.2 = (bf16[128,512]{1,0:T(8,128)(2,1)}, bf16[128,512]{1,0:T(8,128)(2,1)S(1)}, u32[]{:S(2)}, u32[]{:S(2)}) collective-permute-start(bf16[128,512]{1,0:T(8,128)(2,1)} %param.11), channel_id=1, source_target_pairs={{0,8},{8,16},{16,24},{24,32},{32,40},{40,48},{48,56},{56,64},{64,7... | collective-permute-start | bytes 393224 | tf_op jit(solution)/shard_map/ppermute | solution.py:12
  25.1 13.1 %collective-permute-start.3 = (bf16[128,512]{1,0:T(8,128)(2,1)}, bf16[128,512]{1,0:T(8,128)(2,1)S(1)}, u32[]{:S(2)}, u32[]{:S(2)}) collective-permute-start(bf16[128,512]{1,0:T(8,128)(2,1)} %param.11), channel_id=1, source_target_pairs={{8,0},{16,8},{24,16},{32,24},{40,32},{48,40},{56,48},{64,56},{72,6... | collective-permute-start | bytes 393224 | tf_op jit(solution)/shard_map/ppermute | solution.py:12
  29.6 11.2 %collective-permute-start.4 = (bf16[128,512]{1,0:T(8,128)(2,1)}, bf16[128,512]{1,0:T(8,128)(2,1)S(1)}, u32[]{:S(2)}, u32[]{:S(2)}) collective-permute-start(bf16[128,512]{1,0:T(8,128)(2,1)} %param.11), channel_id=1, source_target_pairs={{16,0},{24,8},{32,16},{40,24},{48,32},{56,40},{64,48},{72,56},{80,... | collective-permute-start | bytes 393224 | tf_op jit(solution)/shard_map/ppermute | solution.py:12
  33.0 19.5 %collective-permute-start.5 = (bf16[128,512]{1,0:T(8,128)(2,1)}, bf16[128,512]{1,0:T(8,128)(2,1)S(1)}, u32[]{:S(2)}, u32[]{:S(2)}) collective-permute-start(bf16[128,512]{1,0:T(8,128)(2,1)} %param.11), channel_id=1, source_target_pairs={{24,0},{32,8},{40,16},{48,24},{56,32},{64,40},{72,48},{80,56},{88,... | collective-permute-start | bytes 393224 | tf_op jit(solution)/shard_map/ppermute | solution.py:12
  66.9 33.3 %copy-start.3 = (bf16[128,512]{1,0:T(8,128)(2,1)S(1)}, bf16[128,512]{1,0:T(8,128)(2,1)}, u32[]{:S(2)}) copy-start(bf16[128,512]{1,0:T(8,128)(2,1)} %param.17) | copy-start | bytes 393220
  66.9 33.3 %copy-start.4 = (f32[512]{0:T(512)S(1)}, f32[512]{0:T(512)}, u32[]{:S(2)}) copy-start(f32[512]{0:T(512)} %param.13) | copy-start | bytes 6148
  66.9 63.9 %copy-start.1 = (bf16[16,128,128]{2,1,0:T(8,128)(2,1)S(1)}, bf16[16,128,128]{2,1,0:T(8,128)(2,1)}, u32[]{:S(2)}) copy-start(bf16[16,128,128]{2,1,0:T(8,128)(2,1)} %get-tuple-element.501) | copy-start | bytes 1572868
  66.9 63.9 %all-gather.2.cloned.1.call-start = ((), (), s32[]{:S(2)}) async-start(), calls=%async_computation.3 | async-start | bytes 1179648 | tf_op jit(solution)/shard_map/all_gather | solution.py:81
  103.2 361.3 %all-reduce.2.cloned.1.call-start = ((), (), s32[]{:S(2)}) async-start(), calls=%async_computation.2 | async-start | bytes 2097152 | tf_op jit(solution)/shard_map/psum | solution.py:77
  144.5 27.9 %copy-start.2 = (f32[128,512]{1,0:T(8,128)S(1)}, f32[128,512]{1,0:T(8,128)}, u32[]{:S(2)}) copy-start(f32[128,512]{1,0:T(8,128)} %reduce-scatter.2.cloned.1.call-done) | copy-start | bytes 786436
  145.4 23.1 %collective-permute-start.10 = (f32[128,512]{1,0:T(8,128)S(1)}, f32[128,512]{1,0:T(8,128)S(1)}, u32[]{:S(2)}, u32[]{:S(2)}) collective-permute-start(f32[128,512]{1,0:T(8,128)S(1)} %get-tuple-element.334), channel_id=1, source_target_pairs={{0,16},{8,24},{16,32},{24,40},{32,48},{40,56},{48,64},{56,72},{64,... | collective-permute-start | bytes 786440 | tf_op jit(solution)/shard_map/ppermute | solution.py:12
  150.1 146.8 %collective-permute-start.11 = (f32[128,512]{1,0:T(8,128)}, f32[128,512]{1,0:T(8,128)S(1)}, u32[]{:S(2)}, u32[]{:S(2)}) collective-permute-start(f32[128,512]{1,0:T(8,128)} %get-tuple-element.333), channel_id=1, source_target_pairs={{0,24},{8,32},{16,40},{24,48},{32,56},{40,64},{48,72},{56,80},{64,... | collective-permute-start | bytes 786440 | tf_op jit(solution)/shard_map/ppermute | solution.py:12
  156.1 140.7 %collective-permute-start.6 = (f32[128,512]{1,0:T(8,128)}, f32[128,512]{1,0:T(8,128)}, u32[]{:S(2)}, u32[]{:S(2)}) collective-permute-start(f32[128,512]{1,0:T(8,128)} %get-tuple-element.332), channel_id=1, source_target_pairs={{24,0},{32,8},{40,16},{48,24},{56,32},{64,40},{72,48},{80,56},{88,... | collective-permute-start | bytes 786440 | tf_op jit(solution)/shard_map/ppermute | solution.py:12
  159.8 137.0 %collective-permute-start.7 = (f32[128,512]{1,0:T(8,128)}, f32[128,512]{1,0:T(8,128)}, u32[]{:S(2)}, u32[]{:S(2)}) collective-permute-start(f32[128,512]{1,0:T(8,128)} %get-tuple-element.337), channel_id=1, source_target_pairs={{16,0},{24,8},{32,16},{40,24},{48,32},{56,40},{64,48},{72,56},{80,... | collective-permute-start | bytes 786440 | tf_op jit(solution)/shard_map/ppermute | solution.py:12
  163.2 133.7 %collective-permute-start.8 = (f32[128,512]{1,0:T(8,128)S(1)}, f32[128,512]{1,0:T(8,128)}, u32[]{:S(2)}, u32[]{:S(2)}) collective-permute-start(f32[128,512]{1,0:T(8,128)S(1)} %get-tuple-element.336), channel_id=1, source_target_pairs={{8,0},{16,8},{24,16},{32,24},{40,32},{48,40},{56,48},{64,56},{72,6... | collective-permute-start | bytes 786440 | tf_op jit(solution)/shard_map/ppermute | solution.py:12
  168.5 128.3 %collective-permute-start.9 = (f32[128,512]{1,0:T(8,128)S(1)}, f32[128,512]{1,0:T(8,128)}, u32[]{:S(2)}, u32[]{:S(2)}) collective-permute-start(f32[128,512]{1,0:T(8,128)S(1)} %get-tuple-element.335), channel_id=1, source_target_pairs={{0,8},{8,16},{16,24},{24,32},{32,40},{40,48},{48,56},{56,64},{64,7... | collective-permute-start | bytes 786440 | tf_op jit(solution)/shard_map/ppermute | solution.py:12
Sparse Core Ops, SparseCore 0:
  67.0 33.0 reduce-scatter.1
  103.3 27.4 all-gather.1
  173.8 290.6 all-reduce.1
where the time goes:
time: 474 us; the launch traced here: 473 us
  waiting for transfers between devices  242 us (51%)
  blocking collectives  123 us (26%)
  starting transfers between devices  53.9 us (11%)
  matrix products  19.6 us (4%)
  local copies, waits for them, and re-layouts  16.5 us (3%)
  between operations  14.6 us (3%)
    psum x1, waiting for transfers between devices, body(): grad_weight, grad_bias = lax.psum((weight_term, bias_term), ('row', 'col'))  166 us
    psum x1, blocking collectives, body(): grad_weight, grad_bias = lax.psum((weight_term, bias_term), ('row', 'col'))  123 us
    ppermute x12, starting transfers between devices, passed_along(): return lax.ppermute(block, axis, route)  53.8 us
    reduce_scatter x1, waiting for transfers between devices, body(): lax.psum_scatter(partial_value.reshape(col_count * tile_size, feat_width)...  33.2 us
    all_gather x1, waiting for transfers between devices, body(): lax.all_gather(grad_mid, 'col', axis=0, tiled=True)  27.5 us
    ppermute x12, waiting for transfers between devices, passed_along(): return lax.ppermute(block, axis, route)  15.9 us
  transfers between devices with their start and end apart: 15, of which 6 were waited for; matrix products, arithmetic and copies ran while one was open for 1% of the time, Pallas kernels for 0%

commit v1 on v0

--- a/solution.py
+++ b/solution.py
@@ -2,6 +2,7 @@
 import jax.numpy as jnp
 from jax import lax
 from jax.sharding import PartitionSpec as P
+from jax.lax import psum
 
 REACH = 3
 
@@ -74,7 +75,7 @@
     grad_pre = pullback(cotangent.astype(jnp.float32))[0].astype(jnp.bfloat16)
     weight_term = jnp.einsum("nf,ng->fg", aggregate_b, grad_pre, preferred_element_type=jnp.float32)
     bias_term = jnp.sum(grad_pre.astype(jnp.float32), axis=0)
-    grad_weight, grad_bias = lax.psum((weight_term, bias_term), ("row", "col"))
+    grad_weight, grad_bias = psum(psum((weight_term, bias_term), axis_name="col"), axis_name="row")
     grad_mid = jnp.einsum("ng,fg->nf", grad_pre, weight, preferred_element_type=jnp.float32).astype(
         jnp.bfloat16
     )

time: 474 us -> 431 us (0.909)
  the two profiles are of different devices: /device:TPU:24 before, /device:TPU:32 now
where the time goes in v1:
time: 431 us; the launch traced here: 430 us
  blocking collectives  172 us (40%)
  waiting for transfers between devices  152 us (35%)
  starting transfers between devices  52 us (12%)
  matrix products  19.7 us (5%)
  local copies, waits for them, and re-layouts  16.5 us (4%)
  between operations  14.7 us (3%)
    psum x1, blocking collectives, body(): psum(psum((weight_term, bias_term), axis_name='col'), axis_name='row')  159 us
    psum x1, waiting for transfers between devices, body(): psum((weight_term, bias_term), axis_name='col')  71.1 us
    ppermute x12, starting transfers between devices, passed_along(): return lax.ppermute(block, axis, route)  51.8 us
    reduce_scatter x1, waiting for transfers between devices, body(): lax.psum_scatter(partial_value.reshape(col_count * tile_size, feat_width)...  35 us
    all_gather x1, waiting for transfers between devices, body(): lax.all_gather(grad_mid, 'col', axis=0, tiled=True)  30.8 us
    ppermute x12, waiting for transfers between devices, passed_along(): return lax.ppermute(block, axis, route)  15.1 us
    psum x1, blocking collectives, body(): psum((weight_term, bias_term), axis_name='col')  13.2 us
  transfers between devices with their start and end apart: 16, of which 5 were waited for; matrix products, arithmetic and copies ran while one was open for 4% of the time, Pallas kernels for 0%

profile of v1, /device:TPU:32, one launch (start us, length us, event | category | flops | bytes accessed | tf_op | source)
XLA Modules:
  0.0 430.2 jit_solution(12899982540576874349)
XLA Ops:
  7.2 8.0 %collective-permute-start = (bf16[128,512]{1,0:T(8,128)(2,1)}, bf16[128,512]{1,0:T(8,128)(2,1)S(1)}, u32[]{:S(2)}, u32[]{:S(2)}) collective-permute-start(bf16[128,512]{1,0:T(8,128)(2,1)} %param.11), channel_id=1, source_target_pairs={{0,24},{8,32},{16,40},{24,48},{32,56},{40,64},{48,72},{56,80},{64,... | collective-permute-start | bytes 393224 | tf_op jit(solution)/shard_map/ppermute | solution.py:13
  15.3 6.4 %collective-permute-start.1 = (bf16[128,512]{1,0:T(8,128)(2,1)}, bf16[128,512]{1,0:T(8,128)(2,1)S(1)}, u32[]{:S(2)}, u32[]{:S(2)}) collective-permute-start(bf16[128,512]{1,0:T(8,128)(2,1)} %param.11), channel_id=1, source_target_pairs={{0,16},{8,24},{16,32},{24,40},{32,48},{40,56},{48,64},{56,72},{64,... | collective-permute-start | bytes 393224 | tf_op jit(solution)/shard_map/ppermute | solution.py:13
  21.7 3.4 collective-permute-start.2
  25.1 5.8 %collective-permute-start.3 = (bf16[128,512]{1,0:T(8,128)(2,1)}, bf16[128,512]{1,0:T(8,128)(2,1)S(1)}, u32[]{:S(2)}, u32[]{:S(2)}) collective-permute-start(bf16[128,512]{1,0:T(8,128)(2,1)} %param.11), channel_id=1, source_target_pairs={{8,0},{16,8},{24,16},{32,24},{40,32},{48,40},{56,48},{64,56},{72,6... | collective-permute-start | bytes 393224 | tf_op jit(solution)/shard_map/ppermute | solution.py:13
  30.9 1.9 collective-permute-start.4
  32.8 0.8 add_bitcast_fusion
  34.2 3.0 collective-permute-start.5
  37.3 0.9 bitcast_dynamic-update-slice_fusion.3
  38.2 12.3 %collective-permute-done.4 = bf16[128,512]{1,0:T(8,128)(2,1)S(1)} collective-permute-done((bf16[128,512]{1,0:T(8,128)(2,1)}, bf16[128,512]{1,0:T(8,128)(2,1)S(1)}, u32[]{:S(2)}, u32[]{:S(2)}) %collective-permute-start.4) | collective-permute-done | bytes 131104 | tf_op jit(solution)/shard_map/ppermute | solution.py:13
  50.5 10.3 %while.28 = (s32[]{:T(128)}, f32[8,128,512]{2,0,1:T(8,128)}, s32[16]{0:T(128)S(1)}, bf16[16]{0:T(256)(128)(2,1)S(1)}, bf16[16,128,128]{2,1,0:T(8,128)(2,1)}, /*i...) while((s32[]{:T(128)}, f32[8,128,512]{2,0,1:T(8,128)}, ...), condition=%wide.region_1.0_spmd.clone, body=%wide.region_0.0_spmd.clone.sunk | while | flops 143656096 | bytes 9703877 | solution.py:62
  50.5 0.1 compare_select_fusion.4
  50.6 0.6 gather_fusion
  51.3 1.4 fusion.67
  52.6 0.1 dynamic_slice.80
  52.8 2.1 select_add_fusion.4
  55.0 0.6 gather_fusion
  55.6 1.4 fusion.67
  57.0 0.1 dynamic_slice.80
  57.1 3.7 select_add_fusion.4
  60.8 4.1 copy.18
  65.0 35.0 %reduce-scatter.2.cloned.1.call-done = f32[128,512]{1,0:T(8,128)} async-done(((f32[1024,512]{1,0:T(8,128)}), f32[128,512]{1,0:T(8,128)}) %reduce-scatter.2.cloned.1.call-update) | async-done | bytes 262160 | tf_op jit(solution)/shard_map/reduce_scatter | solution.py:65
  100.0 2.1 convert_reduce_fusion
  102.1 1.3 fusion.43
  103.5 1.0 convolution_convert_fusion
  104.5 71.1 %all-reduce.3.cloned.1.call-done = f32[512,512]{1,0:T(8,128)} async-done(((f32[512,512]{1,0:T(8,128)}), f32[512,512]{1,0:T(8,128)}) %all-reduce.3.cloned.1.call-update) | async-done | bytes 1048592 | tf_op jit(solution)/shard_map/psum | solution.py:78
  175.6 30.8 %all-gather.2.cloned.1.call-done = bf16[1024,512]{1,0:T(8,128)(2,1)} async-done(((bf16[128,512]{1,0:T(8,128)(2,1)}), bf16[1024,512]{1,0:T(8,128)(2,1)}) %all-gather.2.cloned.1.call-update) | async-done | bytes 1048592 | tf_op jit(solution)/shard_map/all_gather | solution.py:82
  206.4 11.0 %while.29 = (s32[]{:T(128)}, f32[7,128,512]{2,0,1:T(8,128)}, s32[16]{0:T(128)S(1)}, bf16[16]{0:T(256)(128)(2,1)S(1)}, bf16[16,128,128]{2,1,0:T(8,128)(2,1)S(1)},...) while((s32[]{:T(128)}, f32[7,128,512]{2,0,1:T(8,128)}, ...), condition=%wide.region_9.0_spmd.clone, body=%wide.region_8.0_spmd.clone.sunk | while | flops 142476432 | bytes 9179589 | solution.py:98
  206.5 1.8 gather_fusion.1
  208.4 0.5 fusion.72
  208.9 0.1 dynamic_slice.84
  209.0 2.1 select_add_fusion.5
  211.2 1.8 gather_fusion.1
  213.1 0.5 fusion.72
  213.6 0.1 dynamic_slice.84
  213.7 3.7 select_add_fusion.5
  217.4 2.7 copy.19
  220.1 0.9 slice_bitcast_fusion.5
  221.0 4.6 %collective-permute-start.10 = (f32[128,512]{1,0:T(8,128)S(1)}, f32[128,512]{1,0:T(8,128)S(1)}, u32[]{:S(2)}, u32[]{:S(2)}) collective-permute-start(f32[128,512]{1,0:T(8,128)S(1)} %get-tuple-element.334), channel_id=1, source_target_pairs={{0,16},{8,24},{16,32},{24,40},{32,48},{40,56},{48,64},{56,72},{64,... | collective-permute-start | bytes 786440 | tf_op jit(solution)/shard_map/ppermute | solution.py:13
  225.7 6.0 %collective-permute-start.11 = (f32[128,512]{1,0:T(8,128)}, f32[128,512]{1,0:T(8,128)S(1)}, u32[]{:S(2)}, u32[]{:S(2)}) collective-permute-start(f32[128,512]{1,0:T(8,128)} %get-tuple-element.333), channel_id=1, source_target_pairs={{0,24},{8,32},{16,40},{24,48},{32,56},{40,64},{48,72},{56,80},{64,... | collective-permute-start | bytes 786440 | tf_op jit(solution)/shard_map/ppermute | solution.py:13
  231.7 4.9 %collective-permute-start.6 = (f32[128,512]{1,0:T(8,128)}, f32[128,512]{1,0:T(8,128)}, u32[]{:S(2)}, u32[]{:S(2)}) collective-permute-start(f32[128,512]{1,0:T(8,128)} %get-tuple-element.332), channel_id=1, source_target_pairs={{24,0},{32,8},{40,16},{48,24},{56,32},{64,40},{72,48},{80,56},{88,... | collective-permute-start | bytes 786440 | tf_op jit(solution)/shard_map/ppermute | solution.py:13
  236.7 3.3 collective-permute-start.7
  240.0 2.5 collective-permute-start.8
  242.5 2.8 collective-permute-done.10
  245.3 1.9 collective-permute-start.9
  247.3 13.2 %psum.30 = f32[512]{0:T(512)S(1)} all-reduce(f32[512]{0:T(512)S(1)} %get-tuple-element.330), channel_id=1, replica_groups=mesh['row'=64,'col'=8] {'col'}, use_global_device_ids=true, to_apply=%region_6.0 | all-reduce | flops 512 | bytes 4096 | tf_op jit(solution)/shard_map/psum | solution.py:78
  260.5 158.8 %psum.31 = f32[512]{0:T(512)} all-reduce(f32[512]{0:T(512)S(1)} %psum.30), channel_id=1, replica_groups=mesh['row'=64,'col'=8] {'row'}, use_global_device_ids=true, to_apply=%region_7.0 | all-reduce | flops 512 | bytes 4096 | tf_op jit(solution)/shard_map/psum | solution.py:78
  419.4 2.0 fusion.42
  421.4 2.3 copy.61
  (49 shorter events, 0.9 us)
Async XLA Ops:
  7.2 92.8 %copy-start = (bf16[512,512]{1,0:T(8,128)(2,1)S(1)}, bf16[512,512]{1,0:T(8,128)(2,1)}, u32[]{:S(2)}) copy-start(bf16[512,512]{1,0:T(8,128)(2,1)} %param.12) | copy-start | bytes 1572868
  7.2 92.8 %reduce-scatter.2.cloned.1.call-start = ((), (), s32[]{:S(2)}) async-start(), calls=%async_computation.1 | async-start | bytes 2359296 | tf_op jit(solution)/shard_map/reduce_scatter | solution.py:65
  7.2 27.0 %collective-permute-start = (bf16[128,512]{1,0:T(8,128)(2,1)}, bf16[128,512]{1,0:T(8,128)(2,1)S(1)}, u32[]{:S(2)}, u32[]{:S(2)}) collective-permute-start(bf16[128,512]{1,0:T(8,128)(2,1)} %param.11), channel_id=1, source_target_pairs={{0,24},{8,32},{16,40},{24,48},{32,56},{40,64},{48,72},{56,80},{64,... | collective-permute-start | bytes 393224 | tf_op jit(solution)/shard_map/ppermute | solution.py:13
  15.3 22.0 %collective-permute-start.1 = (bf16[128,512]{1,0:T(8,128)(2,1)}, bf16[128,512]{1,0:T(8,128)(2,1)S(1)}, u32[]{:S(2)}, u32[]{:S(2)}) collective-permute-start(bf16[128,512]{1,0:T(8,128)(2,1)} %param.11), channel_id=1, source_target_pairs={{0,16},{8,24},{16,32},{24,40},{32,48},{40,56},{48,64},{56,72},{64,... | collective-permute-start | bytes 393224 | tf_op jit(solution)/shard_map/ppermute | solution.py:13
  21.7 15.6 %collective-permute-start.2 = (bf16[128,512]{1,0:T(8,128)(2,1)}, bf16[128,512]{1,0:T(8,128)(2,1)S(1)}, u32[]{:S(2)}, u32[]{:S(2)}) collective-permute-start(bf16[128,512]{1,0:T(8,128)(2,1)} %param.11), channel_id=1, source_target_pairs={{0,8},{8,16},{16,24},{24,32},{32,40},{40,48},{48,56},{56,64},{64,7... | collective-permute-start | bytes 393224 | tf_op jit(solution)/shard_map/ppermute | solution.py:13
  25.1 13.1 %collective-permute-start.3 = (bf16[128,512]{1,0:T(8,128)(2,1)}, bf16[128,512]{1,0:T(8,128)(2,1)S(1)}, u32[]{:S(2)}, u32[]{:S(2)}) collective-permute-start(bf16[128,512]{1,0:T(8,128)(2,1)} %param.11), channel_id=1, source_target_pairs={{8,0},{16,8},{24,16},{32,24},{40,32},{48,40},{56,48},{64,56},{72,6... | collective-permute-start | bytes 393224 | tf_op jit(solution)/shard_map/ppermute | solution.py:13
  30.9 19.6 %collective-permute-start.4 = (bf16[128,512]{1,0:T(8,128)(2,1)}, bf16[128,512]{1,0:T(8,128)(2,1)S(1)}, u32[]{:S(2)}, u32[]{:S(2)}) collective-permute-start(bf16[128,512]{1,0:T(8,128)(2,1)} %param.11), channel_id=1, source_target_pairs={{16,0},{24,8},{32,16},{40,24},{48,32},{56,40},{64,48},{72,56},{80,... | collective-permute-start | bytes 393224 | tf_op jit(solution)/shard_map/ppermute | solution.py:13
  34.2 16.3 %collective-permute-start.5 = (bf16[128,512]{1,0:T(8,128)(2,1)}, bf16[128,512]{1,0:T(8,128)(2,1)S(1)}, u32[]{:S(2)}, u32[]{:S(2)}) collective-permute-start(bf16[128,512]{1,0:T(8,128)(2,1)} %param.11), channel_id=1, source_target_pairs={{24,0},{32,8},{40,16},{48,24},{56,32},{64,40},{72,48},{80,56},{88,... | collective-permute-start | bytes 393224 | tf_op jit(solution)/shard_map/ppermute | solution.py:13
  64.9 35.0 %copy-start.3 = (bf16[128,512]{1,0:T(8,128)(2,1)S(1)}, bf16[128,512]{1,0:T(8,128)(2,1)}, u32[]{:S(2)}) copy-start(bf16[128,512]{1,0:T(8,128)(2,1)} %param.17) | copy-start | bytes 393220
  65.0 35.0 %copy-start.4 = (f32[512]{0:T(512)S(1)}, f32[512]{0:T(512)}, u32[]{:S(2)}) copy-start(f32[512]{0:T(512)} %param.13) | copy-start | bytes 6148
  65.0 110.6 %all-reduce.3.cloned.1.call-start = ((), (), s32[]{:S(2)}) async-start(), calls=%async_computation.2 | async-start | bytes 2097152 | tf_op jit(solution)/shard_map/psum | solution.py:78
  100.0 2.1 copy-start.2
  102.1 104.3 %copy-start.1 = (bf16[16,128,128]{2,1,0:T(8,128)(2,1)S(1)}, bf16[16,128,128]{2,1,0:T(8,128)(2,1)}, u32[]{:S(2)}) copy-start(bf16[16,128,128]{2,1,0:T(8,128)(2,1)} %get-tuple-element.502) | copy-start | bytes 1572868
  103.4 103.0 %all-gather.2.cloned.1.call-start = ((), (), s32[]{:S(2)}) async-start(), calls=%async_computation.4 | async-start | bytes 1179648 | tf_op jit(solution)/shard_map/all_gather | solution.py:82
  104.5 316.9 %all-reduce.5.cloned.1.call-start = ((), (), s32[]{:S(2)}) async-start(), calls=%async_computation.3 | async-start | bytes 2097152 | tf_op jit(solution)/shard_map/psum | solution.py:78
  221.0 24.3 %collective-permute-start.10 = (f32[128,512]{1,0:T(8,128)S(1)}, f32[128,512]{1,0:T(8,128)S(1)}, u32[]{:S(2)}, u32[]{:S(2)}) collective-permute-start(f32[128,512]{1,0:T(8,128)S(1)} %get-tuple-element.334), channel_id=1, source_target_pairs={{0,16},{8,24},{16,32},{24,40},{32,48},{40,56},{48,64},{56,72},{64,... | collective-permute-start | bytes 786440 | tf_op jit(solution)/shard_map/ppermute | solution.py:13
  225.7 193.7 %collective-permute-start.11 = (f32[128,512]{1,0:T(8,128)}, f32[128,512]{1,0:T(8,128)S(1)}, u32[]{:S(2)}, u32[]{:S(2)}) collective-permute-start(f32[128,512]{1,0:T(8,128)} %get-tuple-element.333), channel_id=1, source_target_pairs={{0,24},{8,32},{16,40},{24,48},{32,56},{40,64},{48,72},{56,80},{64,... | collective-permute-start | bytes 786440 | tf_op jit(solution)/shard_map/ppermute | solution.py:13
  231.7 187.6 %collective-permute-start.6 = (f32[128,512]{1,0:T(8,128)}, f32[128,512]{1,0:T(8,128)}, u32[]{:S(2)}, u32[]{:S(2)}) collective-permute-start(f32[128,512]{1,0:T(8,128)} %get-tuple-element.332), channel_id=1, source_target_pairs={{24,0},{32,8},{40,16},{48,24},{56,32},{64,40},{72,48},{80,56},{88,... | collective-permute-start | bytes 786440 | tf_op jit(solution)/shard_map/ppermute | solution.py:13
  236.7 182.7 %collective-permute-start.7 = (f32[128,512]{1,0:T(8,128)}, f32[128,512]{1,0:T(8,128)}, u32[]{:S(2)}, u32[]{:S(2)}) collective-permute-start(f32[128,512]{1,0:T(8,128)} %get-tuple-element.337), channel_id=1, source_target_pairs={{16,0},{24,8},{32,16},{40,24},{48,32},{56,40},{64,48},{72,56},{80,... | collective-permute-start | bytes 786440 | tf_op jit(solution)/shard_map/ppermute | solution.py:13
  240.0 179.4 %collective-permute-start.8 = (f32[128,512]{1,0:T(8,128)S(1)}, f32[128,512]{1,0:T(8,128)}, u32[]{:S(2)}, u32[]{:S(2)}) collective-permute-start(f32[128,512]{1,0:T(8,128)S(1)} %get-tuple-element.336), channel_id=1, source_target_pairs={{8,0},{16,8},{24,16},{32,24},{40,32},{48,40},{56,48},{64,56},{72,6... | collective-permute-start | bytes 786440 | tf_op jit(solution)/shard_map/ppermute | solution.py:13
  245.3 174.0 %collective-permute-start.9 = (f32[128,512]{1,0:T(8,128)S(1)}, f32[128,512]{1,0:T(8,128)}, u32[]{:S(2)}, u32[]{:S(2)}) collective-permute-start(f32[128,512]{1,0:T(8,128)S(1)} %get-tuple-element.335), channel_id=1, source_target_pairs={{0,8},{8,16},{16,24},{24,32},{32,40},{40,48},{48,56},{56,64},{64,7... | collective-permute-start | bytes 786440 | tf_op jit(solution)/shard_map/ppermute | solution.py:13
Sparse Core Ops, SparseCore 0:
  65.1 34.8 reduce-scatter.1
  103.5 72.0 all-reduce.2
  178.4 28.0 all-gather.1
  209.5 198.9 all-reduce.4
